TPU v7x, 32 devices: a whole 2x2x4 slice. The times are simulated.
32 devices in a mesh: prow: 4 (over y, core), pcol: 8 (over z, x).
Axes of the slice: x: 2, y: 2, z: 4, core: 2. Of those that a mesh axis runs over, the one named last changes fastest.
Arguments:
- matrix: float32 [10240, 9216], P('prow', 'pcol'), as said below
- pivots: int32 [1024], replicated, may hold values from 0 to 10239, as said below
Outputs:
- updated: float32 [10240, 9216], P('prow', 'pcol')
Inputs may be any that keep to these rules, and one draw needn't show every extreme that they name: For each i < 1024, pivots[i] is i or a row index of 1024 or more; indices of 1024 or more are distinct. `matrix`: the first 1024 columns hold the factored panel: below the diagonal, the multipliers of the lower factor.
All inputs are finite; a program needn't handle non-finite values.
Results may differ from a plain program's by a relative error of at most 0.000051.
Values sent between devices are 32-bit elements; how exact they have to be, the bound alone decides.
A program may use at most 128 MiB of HBM per device.

v0:
```python
import jax
import jax.numpy as jnp
from jax import lax
from jax.sharding import PartitionSpec as P


def spread(block, axis, owner):
    block = jnp.where(lax.axis_index(axis) == owner, block, jnp.zeros_like(block))
    return lax.psum(block, axis)


def on_device(matrix, pivots):
    row_count = matrix.shape[0]
    col_count = matrix.shape[1]
    panel_width = pivots.shape[0]
    prow_index = lax.axis_index("prow")
    pcol_index = lax.axis_index("pcol")
    panel_rows = spread(matrix[:, :panel_width], "pcol", 0)
    pieces = ((panel_rows, 0, panel_width),)
    owner_prow = pivots // row_count
    local_row = pivots - owner_prow * row_count
    is_mine = (owner_prow == prow_index)[:, None]
    contribution = jnp.where(is_mine, matrix[local_row], 0.0)
    new_top = lax.psum(contribution, "prow")
    old_top = spread(matrix[:panel_width], "prow", 0)

    def solve_top(top_rows):
        return lax.linalg.triangular_solve(
            panel_rows[:panel_width], top_rows, left_side=True, lower=True, unit_diagonal=True
        )

    solved = lax.cond(prow_index == 0, solve_top, jnp.zeros_like, new_top)
    upper_rows = spread(solved, "prow", 0)
    destination = jnp.where(
        (owner_prow == prow_index) & (pivots >= panel_width), local_row, row_count
    )
    swapped = matrix.at[destination].set(old_top, mode="drop")
    piece, begin, finish = pieces[0]
    product = jnp.dot(
        piece, upper_rows, precision=lax.Precision.HIGHEST, preferred_element_type=jnp.float32
    )
    result = swapped - product
    padded_upper = jnp.concatenate(
        [upper_rows, jnp.zeros((row_count - panel_width, col_count), jnp.float32)], axis=0
    )
    global_row = prow_index * row_count + lax.broadcasted_iota(jnp.int32, (row_count, 1), 0)
    result = jnp.where(global_row < panel_width, padded_upper, result)
    global_col = pcol_index * col_count + lax.broadcasted_iota(jnp.int32, (1, col_count), 1)
    return jnp.where(global_col < panel_width, matrix, result)


def solution(mesh):
    return jax.shard_map(
        on_device,
        mesh=mesh,
        in_specs=(P("prow", "pcol"), P()),
        out_specs=P("prow", "pcol"),
        check_vma=False,
    )
```

profile of v0, /device:TPU:31, one launch (start us, length us, event | category | flops | bytes accessed | tf_op | source)
XLA Modules:
  0.0 836.0 jit_solution(6654059166047416843)
XLA Ops:
  6.5 0.0 all-reduce.8.cloned.1.call-start
  6.5 0.7 fusion.35
  7.2 0.7 broadcast_compare_fusion
  7.9 11.0 %gather_fusion = f32[1024,1152]{1,0:T(8,128)} fusion(f32[2560,1152]{1,0:T(8,128)} %param.4, s32[1024]{0:T(1024)S(1)} %get-tuple-element.63), kind=kCustom, calls=%fused_computation | custom fusion | bytes 9441280 | tf_op jit(solution)/shard_map/gather | solution.py:23
  19.0 4.8 broadcast_select_fusion.1
  23.8 0.0 all-reduce.8.cloned.1.call-update
  23.8 0.0 all-reduce.6.cloned.1.call-start
  23.9 10.5 %slice_select_fusion = f32[2560,1024]{1,0:T(8,128)} fusion(f32[2560,1152]{1,0:T(8,128)} %param.4, pred[]{:T(512)S(6)} %eq.17), kind=kLoop, calls=%fused_computation.86 | loop fusion | flops 2621440 | bytes 20971520 | tf_op jit(solution)/shard_map/jit(_where)/select_n | solution.py:8
  34.4 0.0 all-reduce.6.cloned.1.call-update
  34.4 0.0 all-reduce.10.cloned.1.call-start
  34.5 5.0 slice_select_fusion.1
  39.4 78.9 %all-reduce.8.cloned.1.call-done = f32[1024,1152]{1,0:T(8,128)} async-done(((f32[1024,1152]{1,0:T(8,128)}), f32[1024,1152]{1,0:T(8,128)}) %all-reduce.8.cloned.1.call-update) | async-done | bytes 4718608 | tf_op jit(solution)/shard_map/psum | solution.py:24
  118.3 330.0 %all-reduce.6.cloned.1.call-done = f32[2560,1024]{1,0:T(8,128)} async-done(((f32[2560,1024]{1,0:T(8,128)}), f32[2560,1024]{1,0:T(8,128)}) %all-reduce.6.cloned.1.call-update) | async-done | bytes 10485776 | tf_op jit(solution)/shard_map/psum | solution.py:9
  448.3 2.5 conditional.1
  448.3 2.5 broadcast.47
  450.8 2.4 broadcast_select_fusion
  453.2 0.0 all-reduce.10.cloned.1.call-update
  453.2 9.6 %copy.38 = f32[2560,1152]{1,0:T(8,128)} copy(f32[2560,1152]{1,0:T(8,128)} %param.4) | data formatting | bytes 23592960
  462.9 298.7 %all-reduce.10.cloned.1.call-done = (f32[1024,1152]{1,0:T(8,128)}, f32[1024,1152]{1,0:T(8,128)}) async-done(((f32[1024,1152]{1,0:T(8,128)}, f32[1024,1152]{1,0:T(8,128)}), (f32[1024,1152]{1,0:T(8,128)}, f32[1024,1152]{1,0:T(8,128)})) %all-reduce.10.cloned.1.call-update) | async-done | bytes 9437200 | tf_op jit(solution)/shard_map/psum | solution.py:9
  761.5 15.0 %scatter_fusion = f32[2560,1152]{1,0:T(8,128)} fusion(f32[2560,1152]{1,0:T(8,128)} %copy.38, s32[1024]{0:T(1024)S(1)} %get-tuple-element.64, f32[1024,1152]{1,0:T(8,128)} %get-tuple-element.30), kind=kCustom, calls=%fused_computation.1 | custom fusion | bytes 14159872 | tf_op jit(solution)/shard_map/scatter | solution.py:37
  776.5 53.0 %fusion.34 = f32[2560,1152]{1,0:T(8,128)} fusion(f32[2560,1152]{1,0:T(8,128)} %param.4, f32[2560,1152]{1,0:T(8,128)} %scatter_fusion, f32[2560,1024]{1,0:T(8,128)} %all-reduce.6.cloned.1.call-done, f32[1024,1152]{1,0:T(8,128)} %get-tuple-element.31, pred[2560]{0:T(1024)(128)(4,1)S(1)} %add_compare_fusion, pred[1152]{0:T(1024)(128)(4,1)S(1)} %add_compare_fusion.1), kind=kOutput, calls=%fused_computation.85 | convolution fusion | flops 36247633920 | bytes 50597504 | tf_op jit(solution)/shard_map/dot_general | solution.py:39
  (2 shorter events, 0.0 us)
Async XLA Ops:
  6.5 111.8 %all-reduce.8.cloned.1.call-start = ((), (), s32[]{:S(2)}) async-start(), calls=%async_computation.1 | async-start | bytes 9437184 | tf_op jit(solution)/shard_map/psum | solution.py:24
  23.8 424.5 %all-reduce.6.cloned.1.call-start = ((), (), s32[]{:S(2)}) async-start(), calls=%async_computation | async-start | bytes 20971520 | tf_op jit(solution)/shard_map/psum | solution.py:9
  34.4 727.1 %all-reduce.10.cloned.1.call-start = ((), (), s32[]{:S(2)}) async-start(), calls=%async_computation.2 | async-start | bytes 18874368 | tf_op jit(solution)/shard_map/psum | solution.py:9
Sparse Core Ops, SparseCore 0:
  23.9 94.3 all-reduce.7
  122.2 326.0 all-reduce.5
  453.4 308.1 all-reduce.9
where the time goes:
time: 839 us; the launch traced here: 836 us
  waiting for transfers between devices  708 us (84%)
  matrix products  53 us (6%)
  local copies, waits for them, and re-layouts  38.1 us (5%)
  other arithmetic  24.2 us (3%)
  between operations  13.1 us (2%)
    psum x2, waiting for transfers between devices, spread(): return lax.psum(block, axis)  629 us
    psum x1, waiting for transfers between devices, on_device(): new_top = lax.psum(contribution, 'prow')  78.9 us
    dot_general x1, matrix products, on_device(): jnp.dot(piece, upper_rows, precision=lax.Precision.HIGHEST, preferred_ele...  53 us
    select_n x3, other arithmetic, spread(): jnp.where(lax.axis_index(axis) == owner, block, jnp.zeros_like(block))  17.9 us
  transfers between devices with their start and end apart: 3, of which 3 were waited for; matrix products, arithmetic and copies ran while one was open for 3% of the time, Pallas kernels for 0%

commit v1 on v0

v1 whole, which is shorter than its diff:
```python
import functools
import jax
import jax.numpy as jnp
from jax import lax
from jax.experimental import pallas as pl
from jax.experimental.pallas import tpu as pltpu
from jax.sharding import PartitionSpec as P

MESH = pl.DeviceIdType.MESH
CHUNK = 32
BLOCK = 128
F32 = jnp.float32
BF16 = jnp.bfloat16


def exact_dot(a, b):
    return jnp.dot(a, b, precision=lax.Precision.HIGHEST, preferred_element_type=F32)


def plain_dot(a, b):
    return jnp.dot(a, b, preferred_element_type=F32)


def loop(low, high, body, **options):
    def step(i, carry):
        body(i)
        return carry

    lax.fori_loop(low, high, step, 0, **options)


def unit_lower_inverse(block):
    size = block.shape[0]
    row = lax.broadcasted_iota(jnp.int32, (size, size), 0)
    col = lax.broadcasted_iota(jnp.int32, (size, size), 1)
    inverse = jnp.where(row == col, 1.0, 0.0).astype(F32)
    level = 0
    while (1 << level) < size:
        same = (row >> (level + 1)) == (col >> (level + 1))
        below = (((row >> level) & 1) == 1) & (((col >> level) & 1) == 0)
        middle = jnp.where(same & below, block, 0.0)
        if level == 0:
            inverse = inverse - middle
        else:
            inverse = inverse - exact_dot(exact_dot(inverse, middle), inverse)
        level += 1
    return inverse


def kernel(
    nx, nz, ny, pivot_smem, pivot_row, matrix, out,
    mat, panel, new_top, slots, old_top, part0, part1, factor,
    load_sem, a_recv, b_recv, a_send, b_send, row_send, row_recv, top_send, top_recv,
    ld_send, ld_recv, half_send, half_recv, ring_send, ring_recv, store_sem, free_sem,
):
    rows, cols = mat.shape
    width = factor.shape[0]
    half = width // 2
    steps = rows // CHUNK // 2
    head = steps // 5
    ld_steps = width // CHUNK // 2
    prow, pcol = lax.axis_index("prow"), lax.axis_index("pcol")
    y, core = prow // 2, prow % 2
    z, x = pcol // nx, pcol % nx
    source = pcol == 0
    partner = y * 2 + (1 - core)
    y_next = lax.rem(y + 1, ny) * 2 + core
    y_prev = lax.rem(y + ny - 1, ny) * 2 + core

    barrier = pltpu.get_barrier_semaphore()
    has_left, has_right, has_down, has_up = x > 0, x < nx - 1, z > 0, z < nz - 1

    def greet(p, q):
        pl.semaphore_signal(barrier, inc=1, device_id=(p, q), device_id_type=MESH)

    for has, q in ((has_left, pcol - 1), (has_right, pcol + 1), (has_down, pcol - nx), (has_up, pcol + nx)):
        pl.when(has)(functools.partial(greet, prow, q))
    greet(partner, pcol)
    greet(y_next, pcol)
    if ny > 2:
        greet(y_prev, pcol)

    mat_load = pltpu.make_async_copy(matrix, mat, load_sem.at[0])
    mat_load.start()
    panel_load = pltpu.make_async_copy(matrix.at[:, pl.ds(0, width)], panel, load_sem.at[1])
    pl.when(source)(panel_load.start)
    top_load = pltpu.make_async_copy(matrix.at[pl.ds(0, width), :], old_top, load_sem.at[2])
    pl.when(prow == 0)(top_load.start)

    count = sum(h.astype(jnp.int32) for h in (has_left, has_right, has_down, has_up)) + (3 if ny > 2 else 2)
    pl.semaphore_wait(barrier, count)

    def chunk_rows(c, which):
        if which == 0:
            k = jnp.where(c < head, ld_steps * 2 + c, jnp.where(c < head + ld_steps, c - head, c + ld_steps))
        else:
            k = jnp.where(
                c < head, steps + ld_steps + c, jnp.where(c < head + ld_steps, c - head + ld_steps, c + steps)
            )
        return pl.ds(pl.multiple_of(k * CHUNK, CHUNK), CHUNK)

    def copy_to(which, c, way, q):
        recv, send = ((a_recv, a_send), (b_recv, b_send))[which]
        piece = panel.at[chunk_rows(c, which)]
        return pltpu.make_async_remote_copy(
            piece, piece, send.at[way, c], recv.at[c], device_id=(prow, q), device_id_type=MESH
        )

    ways = (
        (
            ((z == 0) & (x < nx - 1), pcol + 1),
            ((x >= 1) & (z < nz - 1), pcol + nx),
            ((x == 1) & (z >= 1), pcol - 1),
        ),
        (
            ((x == 0) & (z < nz - 1), pcol + nx),
            ((z >= 1) & (x < nx - 1), pcol + 1),
            ((z == 1) & (x >= 1), pcol - nx),
        ),
    )

    def forward(c):
        for which in (0, 1):
            pl.when(jnp.logical_not(source))(lambda: copy_to(which, c, 0, pcol).wait_recv())
            for way, (go, q) in enumerate(ways[which]):
                pl.when(go)(lambda: copy_to(which, c, way, q).start())

    def ld_copy(which, c, way, p):
        piece = chunk_rows(c, which)
        slot = which * ld_steps + c - head
        return pltpu.make_async_remote_copy(
            panel.at[piece], factor.at[piece], ld_send.at[way, slot], ld_recv.at[slot],
            device_id=(p, pcol), device_id_type=MESH,
        )

    def spread_factor(c):
        @pl.when(prow == 0)
        def _():
            for which in (0, 1):
                ld_copy(which, c, 0, 1).start()
                ld_copy(which, c, 1, 2).start()

    @pl.when(source)
    def _():
        panel_load.wait()
        loop(0, head, forward)

        @pl.when(prow == 0)
        def _():
            def invert(k):
                begin = pl.multiple_of(k * BLOCK, BLOCK)
                place = (pl.ds(begin, BLOCK), pl.ds(begin, BLOCK))
                panel[place] = unit_lower_inverse(panel[place])

            loop(0, width // BLOCK, invert)

        loop(head, steps, forward)

    top_copy = pltpu.make_async_remote_copy(
        matrix.at[pl.ds(0, width), :], old_top, top_send.at[0], top_recv.at[0],
        device_id=(1, pcol), device_id_type=MESH,
    )
    pl.when(prow == 0)(top_copy.start)
    mat_load.wait()

    def relay(c):
        pl.when(jnp.logical_not(source))(lambda: forward(c))

    per_step = width // head

    def gather_step(c):
        relay(c)

        def one(j):
            i = c * per_step + j
            pivot = pivot_smem[i]
            owner = lax.div(pivot, rows)
            keep = (owner == prow) | ((prow == 0) & (owner >= 2))
            local = jnp.where(owner == prow, pivot - owner * rows, i)
            row = mat[pl.ds(local, 1), :]
            new_top[pl.ds(i, 1), :] = jnp.where(keep, row, 0.0)

        loop(0, per_step, one, unroll=8)

    loop(0, head, gather_step)

    my_half = pl.ds(pl.multiple_of(core * half, half), half)
    other_half = pl.ds(pl.multiple_of((1 - core) * half, half), half)
    half_copy = pltpu.make_async_remote_copy(
        new_top.at[other_half], slots.at[0], half_send.at[0], half_recv.at[0],
        device_id=(partner, pcol), device_id_type=MESH,
    )
    half_copy.start()

    def factor_step(c):
        relay(c)
        spread_factor(c)

    loop(head, head + 2, factor_step)
    half_copy.wait()
    pl.semaphore_signal(free_sem, inc=1, device_id=(partner, pcol), device_id_type=MESH)
    new_top[my_half, :] = new_top[my_half, :] + slots[0]

    def ring_copy(s):
        return pltpu.make_async_remote_copy(
            new_top.at[my_half] if s == 0 else slots.at[s], slots.at[s + 1], ring_send.at[s], ring_recv.at[s],
            device_id=(y_next, pcol), device_id_type=MESH,
        )

    ring_copy(0).start()
    loop(head + 2, head + ld_steps, factor_step)
    after = head + ld_steps
    loop(after, after + 5, relay)

    pivot_col = jnp.transpose(pivot_row[...])[:, 0:1]
    for s in range(ny - 1):
        ring_copy(s).wait_recv()
        if s < ny - 2:
            ring_copy(s + 1).start()
    ring_copy(0).wait_send()

    def combine(h):
        place = pl.ds(h * half, half)
        pivot = pivot_col[h * half:(h + 1) * half]

        def owned(chip):
            return (pivot >= chip * 2 * rows) & (pivot < (chip + 1) * 2 * rows)

        total = jnp.where(owned(y), new_top[place, :], 0.0)
        for s in range(ny - 1):
            origin = lax.rem(y + ny - 1 - s, ny)
            total = jnp.where(owned(origin), slots[s + 1], total)
        new_top[place, :] = total

        @pl.when(y > 0)
        def _():
            for s in range(ny - 1):
                @pl.when(y == s + 1)
                def _():
                    old_top[place, :] = slots[s + 1]

    for h in (0, 1):
        pl.when(core == h)(functools.partial(combine, h))

    new_copy = pltpu.make_async_remote_copy(
        new_top.at[my_half], new_top.at[my_half], half_send.at[1], half_recv.at[1],
        device_id=(partner, pcol), device_id_type=MESH,
    )
    pl.semaphore_wait(free_sem, 1)
    new_copy.start()
    old_copy = pltpu.make_async_remote_copy(
        old_top.at[my_half], old_top.at[my_half], half_send.at[2], half_recv.at[2],
        device_id=(partner, pcol), device_id_type=MESH,
    )
    pl.when(y > 0)(old_copy.start)

    loop(after + 5, after + 8, relay)

    pl.when(y > 0)(old_copy.wait_recv)
    pl.when(prow == 1)(top_copy.wait_recv)
    pl.when(prow == 0)(top_load.wait)

    def split_old(k):
        place = pl.ds(pl.multiple_of(k * BLOCK, BLOCK), BLOCK)
        value = old_top[place, :]
        high = value.astype(BF16)
        part0[place, :] = high
        part1[place, :] = (value - high.astype(F32)).astype(BF16)

    loop(0, width // BLOCK, split_old)

    tile = 256
    tiles = rows // tile
    trailing = (pcol * cols + lax.broadcasted_iota(jnp.int32, (1, cols), 1)) >= width

    def exchange(t):
        place = pl.ds(pl.multiple_of(t * tile, tile), tile)
        ident = prow * rows + t * tile + lax.broadcasted_iota(jnp.int32, (tile, width), 0)
        hit = (pivot_row[0:1, :] == ident) & (ident >= width)
        pick = jnp.where(hit, 1.0, 0.0)
        hits = jnp.sum(pick, axis=1, keepdims=True)
        pick = pick.astype(BF16)
        moved = plain_dot(pick, part0[...]) + plain_dot(pick, part1[...])
        mat[place, :] = jnp.where((hits > 0.5) & trailing, moved, mat[place, :])

    rest_steps = steps - after - 8

    def exchange_step(c):
        relay(c)
        exchange(c - after - 8)

    loop(after + 8, steps, exchange_step)
    loop(rest_steps, tiles, exchange)

    @pl.when(prow > 0)
    def _():
        for slot in range(2 * ld_steps):
            which, c = slot // ld_steps, head + slot % ld_steps
            ld_copy(which, c, 0, prow).wait_recv()

    def relay_chunks(way, p, act):
        def one(slot):
            piece = pl.ds(pl.multiple_of(slot * CHUNK, CHUNK), CHUNK)
            act(pltpu.make_async_remote_copy(
                factor.at[piece], factor.at[piece], ld_send.at[way, slot], ld_recv.at[slot],
                device_id=(p, pcol), device_id_type=MESH,
            ))

        loop(0, 2 * ld_steps, one)

    even = (prow >= 2) & (core == 0)
    pl.when(even)(lambda: relay_chunks(0, prow + 1, lambda d: d.start()))
    onward = even & (y < ny - 1)
    if ny > 2:
        pl.when(onward)(lambda: relay_chunks(1, prow + 2, lambda d: d.start()))

    @pl.when(prow == 0)
    def _():
        local = pltpu.make_async_copy(panel.at[pl.ds(0, width)], factor, load_sem.at[3])
        local.start()
        local.wait()

    new_copy.wait()

    for k in range(width // BLOCK):
        place = pl.ds(k * BLOCK, BLOCK)
        right = new_top[place, :]
        if k:
            right = right - exact_dot(factor[place, pl.ds(0, k * BLOCK)], new_top[pl.ds(0, k * BLOCK), :])
        solved = exact_dot(factor[place, pl.ds(k * BLOCK, BLOCK)], right)
        new_top[place, :] = solved
        high = solved.astype(BF16)
        part0[place, :] = high
        part1[place, :] = (solved - high.astype(F32)).astype(BF16)

    def store(t):
        place = pl.ds(pl.multiple_of(t * tile, tile), tile)
        return pltpu.make_async_copy(mat.at[place], out.at[place], store_sem.at[t])

    def update(t):
        place = pl.ds(pl.multiple_of(t * tile, tile), tile)
        value = panel[place, :]
        high = value.astype(BF16)
        low = (value - high.astype(F32)).astype(BF16)
        product = plain_dot(high, part0[...]) + (plain_dot(high, part1[...]) + plain_dot(low, part0[...]))
        old = mat[place, :]
        mat[place, :] = jnp.where(trailing, old - product, old)
        store(t).start()

    top_tiles = width // tile

    def put_top(t):
        place = pl.ds(pl.multiple_of(t * tile, tile), tile)
        mat[place, :] = jnp.where(trailing, new_top[place, :], mat[place, :])
        store(t).start()

    pl.when(prow == 0)(lambda: loop(0, top_tiles, put_top))
    pl.when(prow > 0)(lambda: loop(0, top_tiles, update))
    loop(top_tiles, tiles, update)
    loop(0, tiles, lambda t: store(t).wait())

    def drain(c):
        for which in (0, 1):
            for way, (go, q) in enumerate(ways[which]):
                pl.when(go)(lambda: copy_to(which, c, way, q).wait_send())

    loop(0, steps, drain)

    @pl.when(prow == 0)
    def _():
        def one(c):
            for which in (0, 1):
                ld_copy(which, c, 0, 1).wait_send()
                ld_copy(which, c, 1, 2).wait_send()

        loop(head, head + ld_steps, one)
        top_copy.wait_send()

    pl.when(even)(lambda: relay_chunks(0, prow + 1, lambda d: d.wait_send()))
    if ny > 2:
        pl.when(onward)(lambda: relay_chunks(1, prow + 2, lambda d: d.wait_send()))
    pl.when(y > 0)(old_copy.wait_send)
    for s in range(1, ny - 1):
        ring_copy(s).wait_send()


def on_device(nx, nz, ny, matrix, pivots):
    rows, cols = matrix.shape
    width = pivots.shape[0]
    steps = rows // CHUNK // 2
    chunks = width // CHUNK
    dma = pltpu.SemaphoreType.DMA
    pivot_row = jnp.broadcast_to(pivots[None, :], (8, width))
    return pl.pallas_call(
        functools.partial(kernel, nx, nz, ny),
        out_shape=jax.ShapeDtypeStruct((rows, cols), F32),
        in_specs=[
            pl.BlockSpec(memory_space=pltpu.SMEM),
            pl.BlockSpec(memory_space=pltpu.VMEM),
            pl.BlockSpec(memory_space=pl.ANY),
        ],
        out_specs=pl.BlockSpec(memory_space=pl.ANY),
        scratch_shapes=[
            pltpu.VMEM((rows, cols), F32),
            pltpu.VMEM((rows, width), F32),
            pltpu.VMEM((width, cols), F32),
            pltpu.VMEM((ny, width // 2, cols), F32),
            pltpu.VMEM((width, cols), F32),
            pltpu.VMEM((width, cols), BF16),
            pltpu.VMEM((width, cols), BF16),
            pltpu.VMEM((width, width), F32),
            dma((4,)),
            dma((steps,)),
            dma((steps,)),
            dma((3, steps)),
            dma((3, steps)),
            dma((1,)),
            dma((1,)),
            dma((1,)),
            dma((1,)),
            dma((2, chunks)),
            dma((chunks,)),
            dma((3,)),
            dma((3,)),
            dma((ny - 1,)),
            dma((ny - 1,)),
            dma((rows // 256,)),
            pltpu.SemaphoreType.REGULAR,
        ],
        compiler_params=pltpu.CompilerParams(
            collective_id=0, has_side_effects=True, vmem_limit_bytes=62 * 1024 * 1024
        ),
    )(pivots, pivot_row, matrix)


def solution(mesh):
    ny = mesh.shape["prow"] // 2
    nz = 4
    nx = mesh.shape["pcol"] // nz
    return jax.shard_map(
        functools.partial(on_device, nx, nz, ny),
        mesh=mesh,
        in_specs=(P("prow", "pcol"), P()),
        out_specs=P("prow", "pcol"),
        check_vma=False,
    )
```

time: 839 us -> 752 us (0.90)
  Pallas kernels: 0 us -> 741 us
  waiting for transfers between devices: 708 us -> 0 us
  matrix products: 53 us -> 0 us
  local copies, waits for them, and re-layouts: 38.1 us -> 10.9 us
  other arithmetic: 24.2 us -> 0 us
  between operations: 13.1 us -> 0.01 us
    pallas_call x0 -> x1, Pallas kernels: none -> 741 us  [on_device(): pl.pallas_call(functools.partial(kernel, nx, nz, ny), out_shape=jax.Shape...]
    psum x3 -> x0, waiting for transfers between devices: 708 us -> none  [the longest x2 629 us: spread(): return lax.psum(block, axis)]
    dot_general x1 -> x0, matrix products: 53 us -> none  [on_device(): jnp.dot(piece, upper_rows, precision=lax.Precision.HIGHEST, preferred_ele...]
    select_n x4 -> x0, other arithmetic: 22.7 us -> none  [the longest x3 17.9 us: spread(): jnp.where(lax.axis_index(axis) == owner, block, jnp.zeros_like(block))]
    scatter x1 -> x0, local copies, waits for them, and re-layouts: 15 us -> none  [on_device(): swapped = matrix.at[destination].set(old_top, mode='drop')]
    gather x1 -> x0, local copies, waits for them, and re-layouts: 11 us -> none  [on_device(): contribution = jnp.where(is_mine, matrix[local_row], 0.0)]
  transfers between devices with their start and end apart: 3 -> 0, of which waited for: 3 -> 0; matrix products, arithmetic and copies ran while one was open for 3% -> 0% of each run, Pallas kernels for 0% -> 0%
where the time goes in v1:
time: 752 us
  Pallas kernels  741 us (99%)
  local copies, waits for them, and re-layouts  10.9 us (1%)
    pallas_call x1, Pallas kernels, on_device(): pl.pallas_call(functools.partial(kernel, nx, nz, ny), out_shape=jax.Shape...  741 us

profile of v1, /device:TPU:31, one launch (start us, length us, event | category | flops | bytes accessed | tf_op | source)
XLA Modules:
  0.0 752.2 jit_solution(5972425572754173734)
XLA Ops:
  0.0 1.3 broadcast_in_dim.2.pivot_row
  1.3 741.3 %shard_map.28 = f32[2560,1152]{1,0:T(8,128)} custom-call(s32[1024]{0:T(1024)} %pivot_smem.1, s32[8,1024]{1,0:T(8,128)} %broadcast_in_dim.2.pivot_row, f32[2560,1152]{1,0:T(8,128)} %matrix.1), custom_call_target="tpu_custom_call" | custom-call | tf_op jit(solution)/shard_map/pallas_call | solution.py:394
  742.6 9.6 %copy.4 = f32[2560,1152]{1,0:T(8,128)} copy(f32[2560,1152]{1,0:T(8,128)} %shard_map.28) | data formatting | bytes 23592960

commit v2 on v1

--- a/solution.py
+++ b/solution.py
@@ -119,12 +119,6 @@
         ),
     )
 
-    def forward(c):
-        for which in (0, 1):
-            pl.when(jnp.logical_not(source))(lambda: copy_to(which, c, 0, pcol).wait_recv())
-            for way, (go, q) in enumerate(ways[which]):
-                pl.when(go)(lambda: copy_to(which, c, way, q).start())
-
     def ld_copy(which, c, way, p):
         piece = chunk_rows(c, which)
         slot = which * ld_steps + c - head
@@ -133,17 +127,38 @@
             device_id=(p, pcol), device_id_type=MESH,
         )
 
-    def spread_factor(c):
-        @pl.when(prow == 0)
+    def forward(which, c):
+        for way, (go, q) in enumerate(ways[which]):
+            pl.when(go)(lambda: copy_to(which, c, way, q).start())
+
+        @pl.when((prow == 0) & (c >= head) & (c < head + ld_steps))
         def _():
-            for which in (0, 1):
-                ld_copy(which, c, 0, 1).start()
-                ld_copy(which, c, 1, 2).start()
+            ld_copy(which, c, 0, 1).start()
+            ld_copy(which, c, 1, 2).start()
+
+    def send_both(c):
+        forward(0, c)
+        forward(1, c)
+
+    depths = (
+        jnp.where(z == 0, x, jnp.where(x == 0, z + 2, z + x)),
+        jnp.where(x == 0, z, jnp.where(z == 0, x + 2, z + x)),
+    )
+    all_steps = steps + 2 * max(nx + nz - 2, nx + 1, nz + 1)
+
+    def relay(step):
+        for which in (0, 1):
+            c = step - 2 * depths[which]
+
+            @pl.when(jnp.logical_not(source) & (c >= 0) & (c < steps))
+            def _():
+                copy_to(which, c, 0, pcol).wait_recv()
+                forward(which, c)
 
     @pl.when(source)
     def _():
         panel_load.wait()
-        loop(0, head, forward)
+        loop(0, head, send_both)
 
         @pl.when(prow == 0)
         def _():
@@ -154,7 +169,7 @@
 
             loop(0, width // BLOCK, invert)
 
-        loop(head, steps, forward)
+        loop(head, steps, send_both)
 
     top_copy = pltpu.make_async_remote_copy(
         matrix.at[pl.ds(0, width), :], old_top, top_send.at[0], top_recv.at[0],
@@ -162,9 +177,6 @@
     )
     pl.when(prow == 0)(top_copy.start)
     mat_load.wait()
-
-    def relay(c):
-        pl.when(jnp.logical_not(source))(lambda: forward(c))
 
     per_step = width // head
 
@@ -192,11 +204,7 @@
     )
     half_copy.start()
 
-    def factor_step(c):
-        relay(c)
-        spread_factor(c)
-
-    loop(head, head + 2, factor_step)
+    loop(head, head + 2, relay)
     half_copy.wait()
     pl.semaphore_signal(free_sem, inc=1, device_id=(partner, pcol), device_id_type=MESH)
     new_top[my_half, :] = new_top[my_half, :] + slots[0]
@@ -208,7 +216,7 @@
         )
 
     ring_copy(0).start()
-    loop(head + 2, head + ld_steps, factor_step)
+    loop(head + 2, head + ld_steps, relay)
     after = head + ld_steps
     loop(after, after + 5, relay)
 
@@ -283,14 +291,12 @@
         moved = plain_dot(pick, part0[...]) + plain_dot(pick, part1[...])
         mat[place, :] = jnp.where((hits > 0.5) & trailing, moved, mat[place, :])
 
-    rest_steps = steps - after - 8
-
     def exchange_step(c):
         relay(c)
         exchange(c - after - 8)
 
-    loop(after + 8, steps, exchange_step)
-    loop(rest_steps, tiles, exchange)
+    loop(after + 8, after + 8 + tiles, exchange_step)
+    loop(after + 8 + tiles, all_steps, relay)
 
     @pl.when(prow > 0)
     def _():

time: 752 us -> 204 us (0.27)
  the two profiles are of different devices: /device:TPU:31 before, /device:TPU:5 now
where the time goes in v2:
time: 204 us
  Pallas kernels  193 us (95%)
  local copies, waits for them, and re-layouts  10.9 us (5%)
    pallas_call x1, Pallas kernels, on_device(): pl.pallas_call(functools.partial(kernel, nx, nz, ny), out_shape=jax.Shape...  193 us
    unnamed x1, local copies, waits for them, and re-layouts  9.63 us

profile of v2, /device:TPU:5, one launch (start us, length us, event | category | flops | bytes accessed | tf_op | source)
XLA Modules:
  0.0 204.2 jit_solution(4025539976713570975)
XLA Ops:
  0.0 1.3 broadcast_in_dim.2.pivot_row
  1.3 193.3 %shard_map.28 = f32[2560,1152]{1,0:T(8,128)} custom-call(s32[1024]{0:T(1024)} %pivot_smem.1, s32[8,1024]{1,0:T(8,128)} %broadcast_in_dim.2.pivot_row, f32[2560,1152]{1,0:T(8,128)} %matrix.1), custom_call_target="tpu_custom_call" | custom-call | tf_op jit(solution)/shard_map/pallas_call | solution.py:400
  194.6 9.6 %copy.4 = f32[2560,1152]{1,0:T(8,128)} copy(f32[2560,1152]{1,0:T(8,128)} %shard_map.28) | data formatting | bytes 23592960
